TPU v7x, 256 devices: a whole 4x4x8 slice. The times are simulated.
256 devices in a mesh: seq: 64 (over y, z, core), head: 4 (over x).
Axes of the slice: x: 4, y: 4, z: 8, core: 2. Of those that a mesh axis runs over, the one named last changes fastest.
Arguments:
- queries: float32 [8192, 2048], P('seq', 'head'), may hold values from -6 to 6
- keys: float32 [8192, 2048], P('seq', 'head'), may hold values from -6 to 6
- values: float32 [8192, 2048], P('seq', 'head'), may hold values from -6 to 6
- rates: float32 [4, 8192], P('head', 'seq'), may hold values from 0.05 to 1
- gate_fast: float32 [4, 512, 512], P('head'), may hold values from -0.25 to 0.25
- up_fast: float32 [4, 512, 512], P('head'), may hold values from -0.25 to 0.25
- down_fast: float32 [4, 512, 512], P('head'), may hold values from -0.25 to 0.25
- out_proj: bfloat16 [2048, 4096], P('head', 'seq'), may hold values from -0.125 to 0.125
- out_grad: bfloat16 [8192, 4096], P('seq', 'head'), may hold values from -6 to 6
Outputs:
- query_grad: float32 [8192, 2048], P('seq', 'head')
- key_grad: float32 [8192, 2048], P('seq', 'head')
- value_grad: float32 [8192, 2048], P('seq', 'head')
- gate_grad: float32 [4, 512, 512], P('head', 'seq')
- up_grad: float32 [4, 512, 512], P('head', 'seq')
- down_grad: float32 [4, 512, 512], P('head', 'seq')
All inputs are finite; a program needn't handle non-finite values.
Results may differ from a plain program's by a relative error of at most 0.0003.
Values may be sent and summed in bfloat16 or wider, within the bound.
A program may use at most 64 MiB of HBM per device.

v0:
```python
import math

import jax
import jax.numpy as jnp
from jax import lax
from jax.experimental import pallas as pl
from jax.experimental.pallas import tpu as pltpu
from jax.sharding import Mesh
from jax.sharding import PartitionSpec as P

MESH = pl.DeviceIdType.MESH
SEQ = ("y", "z", "c")
F32 = jnp.float32
BF16 = jnp.bfloat16
NY, NZ, NC, NX = 4, 8, 2, 4
TOK = 128
D = 512
FS = 64
SCALE = 0.3 * math.sqrt(512)
EPS = 1e-06


def halves(x):
    hi = x.astype(BF16)
    return hi, (x - hi.astype(F32)).astype(BF16)


def dot_nt(a, b):
    return lax.dot_general(a, b, (((1,), (1,)), ((), ())), preferred_element_type=F32)


def dot_nn(a, b):
    return lax.dot_general(a, b, (((1,), (0,)), ((), ())), preferred_element_type=F32)


def dot_tn(a, b):
    return lax.dot_general(a, b, (((0,), (0,)), ((), ())), preferred_element_type=F32)


def three(product, a, b_hi, b_lo):
    hi, lo = halves(a)
    n = a.shape[0]
    both = product(jnp.concatenate([hi, lo], axis=0), b_hi)
    return both[:n] + both[n:] + product(hi, b_lo)


def back(acts, mats):
    a_hi, a_lo = halves(acts)
    m_hi, m_lo = halves(mats)
    return dot_tn(
        jnp.concatenate([a_hi, a_lo, a_hi], axis=0), jnp.concatenate([m_hi, m_hi, m_lo], axis=0)
    )


def row_sum(x):
    return jnp.sum(x, axis=1, keepdims=True)


def col_sum(x):
    return jnp.sum(x, axis=0, keepdims=True)


def total(x):
    return jnp.sum(jnp.sum(x, axis=1, keepdims=True), axis=0, keepdims=True)


def kernel(
    q_ref, k_ref, v_ref, rate_ref, g_hbm, u_hbm, w_hbm, oproj_ref, ograd_ref,
    qg_ref, kg_ref, vg_ref, gg_ref, ug_ref, dg_ref,
    k2, t2, q2, o2, oproj_sib, ochunk, oall, grads,
    gs, us, wcol, wts,
    before_s, linear_s, hgrad_s,
    s1, r1, a1, st1, sty1, sts1, stz1,
    s2, r2, a2, st2, sty2, sts2, stz2,
    s3, r3, d3, rd3, ds3, dr3,
    part_q, sib_q, sum_q, rec_q, part_k, sib_k, sum_k, rec_k, part_t, sib_t, sum_t, rec_t,
    sems, lsem,
):
    y, z, c, x = (lax.axis_index(name) for name in ("y", "z", "c", "head"))
    used = [0]

    def at_y(dy, other=False):
        return (lax.rem(y + dy, NY), z, 1 - c if other else c, x)

    def at_z(dz):
        return (y, lax.rem(z + dz, NZ), c, x)

    def at_x(dx):
        return (y, z, c, lax.rem(x + dx, NX))

    sibling = (y, z, 1 - c, x)
    y_order = (1, 3, 2)
    z_order = (4, 3, 5, 2, 6, 1, 7)

    def send(src, dst, device):
        i = used[0]
        used[0] += 2
        copy = pltpu.make_async_remote_copy(
            src_ref=src, dst_ref=dst, send_sem=sems.at[i], recv_sem=sems.at[i + 1],
            device_id=device, device_id_type=MESH,
        )
        copy.start()
        started.append(copy)
        return copy

    started = []

    def arrived(copies):
        for copy in copies:
            copy.wait_recv()

    loads = []
    for i, (src, dst) in enumerate(
        (
            (g_hbm.at[y, :, c], gs),
            (u_hbm.at[y, :, c], us),
            (w_hbm.at[:, pl.ds(pl.multiple_of(y * 128, 128), 128)], wcol),
        )
    ):
        copy = pltpu.make_async_copy(src, dst, lsem.at[i])
        copy.start()
        loads.append(copy)

    barrier = pltpu.get_barrier_semaphore()
    partners = [sibling]
    partners += [at_y(d) for d in (1, 2, 3)] + [at_y(d, True) for d in (1, 2, 3)]
    partners += [at_z(d) for d in range(1, NZ)] + [at_x(d) for d in (1, 2, 3)]
    for device in partners:
        pl.semaphore_signal(barrier, inc=1, device_id=device, device_id_type=MESH)
    pl.semaphore_wait(barrier, len(partners))

    me = 2 * y + c

    osib = send(
        oproj_ref.at[pl.ds(pl.multiple_of((1 - c) * 256, 256), 256)], oproj_sib, sibling
    )
    tokens = pl.ds(pl.multiple_of(c * TOK, TOK), TOK)
    grads[x, tokens, :] = ograd_ref[...]
    xs = [send(grads.at[x, tokens], grads.at[x, tokens], at_x(d)) for d in (1, 3, 2)]
    gsib = [send(grads.at[x, tokens], grads.at[x, tokens], sibling)]

    def place(buffer, value):
        hi, lo = halves(value)
        buffer[me, 0] = hi
        buffer[me, 1] = lo

    def to_y(buffer):
        return [send(buffer.at[me], buffer.at[me], at_y(d)) for d in y_order]

    def forward(buffer, copies):
        result = []
        for d, copy in zip(y_order, copies):
            copy.wait_recv()
            block = 2 * lax.rem(y + NY - d, NY) + c
            result.append(send(buffer.at[block], buffer.at[block], sibling))
        return result

    place(k2, k_ref[...])
    ky = to_y(k2)
    rate_cols = jnp.broadcast_to(rate_ref[...], (TOK, TOK)).T
    rate_full = jnp.concatenate([rate_cols] * 4, axis=1)
    place(t2, -(rate_full * v_ref[...]))
    ty = to_y(t2)
    ksib = [send(k2.at[me], k2.at[me], sibling)]
    tsib = [send(t2.at[me], t2.at[me], sibling)]

    osib.wait_recv()
    own = oproj_ref[pl.ds(pl.multiple_of(c * 256, 256), 256), :].astype(F32)
    other = oproj_sib[...].astype(F32)
    first = c == 0
    ochunk[...] = jnp.concatenate(
        [jnp.where(first, own, other), jnp.where(first, other, own)], axis=1
    ).astype(BF16)
    zcols = pl.ds(pl.multiple_of(z * 128, 128), 128)
    oall[y, :, zcols] = ochunk[...]
    oz = [send(ochunk, oall.at[y, :, zcols], at_z(d)) for d in z_order]

    place(q2, q_ref[...])
    for copy in loads:
        copy.wait()
    wt = wcol[...].T.reshape(NZ, 2, 8, D)
    wts[...] = jnp.where(first, wt[:, 0], wt[:, 1])

    ksib += forward(k2, ky)
    tsib += forward(t2, ty)

    arrived(oz)
    oy = [send(oall.at[y], oall.at[y], at_y(d)) for d in y_order]
    arrived(ksib)
    arrived(tsib)

    def flat(ref):
        return ref[...].reshape(FS, D)

    def whole(buffer):
        return tuple(buffer[:, i].reshape(8 * TOK, D) for i in (0, 1))

    def silu_parts(before):
        sigma = jax.nn.sigmoid(before)
        return sigma, before * sigma, sigma * (1.0 + before * (1.0 - sigma))

    with jax.named_scope("partials"):
        both = three(dot_nt, jnp.concatenate([flat(gs), flat(us)], axis=0), *whole(k2))
        before, linear = both[:FS], both[FS:]
        hgrad = three(dot_nt, flat(wts), *whole(t2))
        before_s[...] = before
        linear_s[...] = linear
        hgrad_s[...] = hgrad
        sigma, act, dsilu = silu_parts(before)
        pgu = three(
            dot_nn, jnp.concatenate([hgrad * linear * dsilu, hgrad * act], axis=0), *whole(k2)
        )
        pd = three(dot_nn, act * linear, *whole(t2))
        s1[:, 0:8] = pgu[:FS].reshape(NZ, 8, D)
        s1[:, 8:16] = pgu[FS:].reshape(NZ, 8, D)
        s1[:, 16:24] = pd.reshape(NZ, 8, D)

    def scatter_z(src, dst):
        return [
            send(src.at[lax.rem(z + d, NZ)], dst.at[z], at_z(d)) for d in z_order
        ]

    def gather_z(buffer):
        return [send(buffer.at[z], buffer.at[z], at_z(d)) for d in z_order]

    def summed_z(src, dst, copies):
        value = src[z]
        for d, copy in zip(z_order, copies):
            copy.wait_recv()
            value = value + dst[lax.rem(z + NZ - d, NZ)]
        return value

    def plane_sum(st, sty, sts, stz, value):
        st[...] = value
        sends = [send(st, sty.at[me], sibling)]
        sends += [send(st, sty.at[me], at_y(d)) for d in (1, 2, 3)]
        sends += [send(st, sty.at[me], at_y(d, True)) for d in (1, 2, 3)]
        sty[me] = value
        arrived(sends)
        group = jnp.sum(sty[...], axis=0)
        sts[...] = group
        stz[z] = group
        sends = [send(sts, stz.at[z], at_z(d)) for d in z_order]
        return sends

    rs1 = scatter_z(s1, r1)

    for d, copy in zip((1, 3, 2), xs):
        copy.wait_recv()
        src = lax.rem(x + NX - d, NX)
        gsib.append(send(grads.at[src, tokens], grads.at[src, tokens], sibling))

    chunk = summed_z(s1, r1, rs1)
    a1[z] = chunk
    ag1 = gather_z(a1)
    gc, uc, wc = gs[z], us[z], wts[z]
    pg_c, pu_c, pd_c = chunk[0:8], chunk[8:16], chunk[16:24]
    zs1 = plane_sum(
        st1, sty1, sts1, stz1,
        jnp.concatenate(
            [
                col_sum(pg_c * pg_c), col_sum(pu_c * pu_c), col_sum(pd_c * pd_c),
                col_sum(wc * pd_c), col_sum(wc * wc), jnp.zeros((3, D), F32),
            ],
            axis=0,
        ),
    )
    qy = to_y(q2)
    qsib = [send(q2.at[me], q2.at[me], sibling)]

    arrived(gsib)
    arrived(oy)
    cot = dot_nt(grads[0], oall[0])
    for i in (1, 2, 3):
        cot = cot + dot_nt(grads[i], oall[i])
    cot_hi, cot_lo = halves(cot)
    cols = pl.ds(pl.multiple_of(c * 256, 256), 256)
    rows = pl.ds(2 * y, 2)
    o2[rows, 0, :, cols] = cot_hi.reshape(2, TOK, 256)
    o2[rows, 1, :, cols] = cot_lo.reshape(2, TOK, 256)
    here = o2.at[rows, :, :, cols]
    coty = [send(here, here, at_y(d)) for d in y_order]
    cotsib = [send(here, here, sibling)]

    qsib += forward(q2, qy)
    for d, copy in zip(y_order, coty):
        copy.wait_recv()
        there = o2.at[pl.ds(2 * lax.rem(y + NY - d, NY), 2), :, :, cols]
        cotsib.append(send(there, there, sibling))

    arrived(zs1)
    arrived(ag1)

    with jax.named_scope("renormed"):
        stats = jnp.sum(stz1[...], axis=0)
        pn_g = jnp.sqrt(total(stats[0:1]) + EPS)
        pn_u = jnp.sqrt(total(stats[1:2]) + EPS)
        pn_d = jnp.sqrt(total(stats[2:3]) + EPS)
        k_g, k_u, k_d = SCALE / pn_g, SCALE / pn_u, SCALE / pn_d
        d_pp, d_wp, d_ww = stats[2:3], stats[3:4], stats[4:5]
        old_d = jnp.sqrt(d_ww + EPS)
        new_d = jnp.sqrt(
            jnp.maximum(d_ww - 2.0 * k_d * d_wp + k_d * k_d * d_pp, 0.0) + EPS
        )
        d_pm = d_wp - k_d * d_pp

        def moved_rows(matrix, partial, k):
            moved = matrix - partial * k
            old = jnp.sqrt(row_sum(matrix * matrix) + EPS)
            new = jnp.sqrt(row_sum(moved * moved) + EPS)
            return moved, old, new

        g_m, u_m, w_m = flat(gs), flat(us), flat(wts)
        p_g = a1[:, 0:8].reshape(FS, D)
        p_u = a1[:, 8:16].reshape(FS, D)
        p_d = a1[:, 16:24].reshape(FS, D)
        mv_g, old_g, new_g = moved_rows(g_m, p_g, k_g)
        mv_u, old_u, new_u = moved_rows(u_m, p_u, k_u)
        mv_d = w_m - p_d * k_d
        ren_gu = jnp.concatenate([mv_g * (old_g / new_g), mv_u * (old_u / new_u)], axis=0)
        ren_d = mv_d * (old_d / new_d)

    arrived(qsib)
    arrived(cotsib)
    with jax.named_scope("cotangents"):
        both = three(dot_nt, ren_gu, *whole(q2))
        before, linear = both[:FS], both[FS:]
        hcot = three(dot_nt, ren_d, *whole(o2))
        sigma, act, dsilu = silu_parts(before)
        acts_q = jnp.concatenate([hcot * linear * dsilu, hcot * act], axis=0)
        cgu = three(dot_nn, acts_q, *whole(q2))
        cd = three(dot_nn, act * linear, *whole(o2))
        s2[:, 0:8] = cgu[:FS].reshape(NZ, 8, D)
        s2[:, 8:16] = cgu[FS:].reshape(NZ, 8, D)
        s2[:, 16:24] = cd.reshape(NZ, 8, D)
    rs2 = scatter_z(s2, r2)
    with jax.named_scope("query_grad"):
        part_q[...] = back(acts_q, ren_gu).reshape(NY, 2, TOK, D)
    sibq = send(part_q.at[:, 1 - c], sib_q, sibling)

    chunk2 = summed_z(s2, r2, rs2)
    a2[z] = chunk2
    ag2 = gather_z(a2)

    def row_back(matrix, partial, k, grad):
        moved, old, new = moved_rows(matrix, partial, k)
        along = row_sum(moved * grad)
        moved_grad = (old / new) * (grad - moved * (along / (new * new)))
        return moved_grad, moved_grad + (along / (new * old)) * matrix

    cg_c, cu_c, cd_c = chunk2[0:8], chunk2[8:16], chunk2[16:24]
    mg_c, direct_g = row_back(gc, pg_c, k_g, cg_c)
    mu_c, direct_u = row_back(uc, pu_c, k_u, cu_c)
    zs2 = plane_sum(
        st2, sty2, sts2, stz2,
        jnp.concatenate(
            [
                -col_sum(pg_c * mg_c), -col_sum(pu_c * mu_c),
                col_sum((wc - pd_c * k_d) * cd_c), col_sum(pd_c * cd_c),
                jnp.zeros((4, D), F32),
            ],
            axis=0,
        ),
    )

    def to_owner(part, sib, summed, rec, copy):
        copy.wait_recv()
        summed[...] = part[:, c] + sib[...]
        return [
            send(summed.at[lax.rem(y + d, NY)], rec.at[y], at_y(d)) for d in y_order
        ]

    def owned(summed, rec, copies):
        value = summed[y]
        for d, copy in zip(y_order, copies):
            copy.wait_recv()
            value = value + rec[lax.rem(y + NY - d, NY)]
        return value

    yq = to_owner(part_q, sib_q, sum_q, rec_q, sibq)

    arrived(zs2)
    arrived(ag2)
    with jax.named_scope("direction"):
        stats2 = jnp.sum(stz2[...], axis=0)
        inner_g, inner_u = total(stats2[0:1]), total(stats2[1:2])
        along_d, d_pg = stats2[2:3], stats2[3:4]
        ratio_d = old_d / new_d
        shrink_d = along_d / (new_d * new_d)
        inner_d = -total(ratio_d * (d_pg - d_pm * shrink_d))
        c_g = a2[:, 0:8].reshape(FS, D)
        c_u = a2[:, 8:16].reshape(FS, D)
        c_d = a2[:, 16:24].reshape(FS, D)
        mgrad_g, _ = row_back(g_m, p_g, k_g, c_g)
        mgrad_u, _ = row_back(u_m, p_u, k_u, c_u)
        mgrad_d = ratio_d * (c_d - mv_d * shrink_d)
        direct_d = mgrad_d + (along_d / (new_d * old_d)) * w_m
        dir_g = -k_g * (mgrad_g + p_g * (inner_g / (pn_g * pn_g)))
        dir_u = -k_u * (mgrad_u + p_u * (inner_u / (pn_u * pn_u)))
        dir_d = -k_d * (mgrad_d + p_d * (inner_d / (pn_d * pn_d)))

    with jax.named_scope("through"):
        both = three(dot_nt, jnp.concatenate([dir_g, dir_u], axis=0), *whole(k2))
        d_bg, d_lg = both[:FS], both[FS:]
        d_hid = three(dot_nt, dir_d, *whole(t2))
        before, linear, hgrad = before_s[...], linear_s[...], hgrad_s[...]
        sigma, act, dsilu = silu_parts(before)
        curve = sigma * (1.0 - sigma) * (2.0 + before * (1.0 - 2.0 * sigma))
        d_h = d_bg * linear * dsilu + d_lg * act
        d_l = d_bg * hgrad * dsilu + d_hid * act
        d_b = d_bg * hgrad * linear * curve + (d_lg * hgrad + d_hid * linear) * dsilu
        part_t[...] = back(
            jnp.concatenate([act * linear, d_h], axis=0),
            jnp.concatenate([dir_d, w_m], axis=0),
        ).reshape(NY, 2, TOK, D)
        sibt = send(part_t.at[:, 1 - c], sib_t, sibling)
        part_k[...] = back(
            jnp.concatenate([hgrad * linear * dsilu, hgrad * act, d_b, d_l], axis=0),
            jnp.concatenate([dir_g, dir_u, g_m, u_m], axis=0),
        ).reshape(NY, 2, TOK, D)
        sibk = send(part_k.at[:, 1 - c], sib_k, sibling)
        yt = to_owner(part_t, sib_t, sum_t, rec_t, sibt)
        th_d = three(dot_nn, d_h, *whole(t2))
        th_d = th_d + jnp.where(z == 0, direct_d, jnp.zeros_like(direct_d))
        th_d = th_d.reshape(NZ, 1, 8, D)
        none = jnp.zeros_like(th_d)
        th_d = jnp.concatenate(
            [jnp.where(first, th_d, none), jnp.where(first, none, th_d)], axis=1
        ).reshape(2 * FS, D)
        th_t = th_d.T.reshape(NY, NZ, 2, 8, 2 * FS)
        for i in range(NZ):
            d3[i] = th_t[:, i].reshape(8, 8, 2 * FS)
        rsd = scatter_z(d3, rd3)
        yk = to_owner(part_k, sib_k, sum_k, rec_k, sibk)
        th_gu = three(dot_nn, jnp.concatenate([d_b, d_l], axis=0), *whole(k2))
        s3[:, 0:8] = th_gu[:FS].reshape(NZ, 8, D)
        s3[:, 8:16] = th_gu[FS:].reshape(NZ, 8, D)
        rs3 = scatter_z(s3, r3)

    qg_ref[...] = owned(sum_q, rec_q, yq)
    down = summed_z(d3, rd3, rsd)
    ds3[...] = down
    dr3[me] = ds3[me]
    fin = [send(ds3.at[2 * y + 1 - c], dr3.at[me], sibling)]
    for d in (1, 2, 3):
        to = 2 * lax.rem(y + d, NY)
        fin.append(send(ds3.at[to + c], dr3.at[me], at_y(d)))
        fin.append(send(ds3.at[to + 1 - c], dr3.at[me], at_y(d, True)))
    vg_ref[...] = -(rate_full * owned(sum_t, rec_t, yt))
    kg_ref[...] = owned(sum_k, rec_k, yk)
    gate_up = summed_z(s3, r3, rs3)
    gg_ref[...] = gate_up[0:8] + direct_g
    ug_ref[...] = gate_up[8:16] + direct_u
    arrived(fin)
    dg_ref[...] = jnp.concatenate(
        [dr3[2 * i] + dr3[2 * i + 1] for i in range(NY)], axis=1
    )
    for copy in started:
        copy.wait_send()


def body(queries, keys, values, rates, gate_fast, up_fast, down_fast, out_proj, out_grad):
    vmem = pl.BlockSpec(memory_space=pltpu.VMEM)
    hbm = pl.BlockSpec(memory_space=pl.ANY)

    def buf(*shape, dtype=F32):
        return pltpu.VMEM(shape, dtype)

    exchange = [buf(NZ, 24, D)] * 3 + [buf(8, D), buf(8, 8, D), buf(8, D), buf(NZ, 8, D)]
    grads = [buf(NY, 2, TOK, D), buf(NY, TOK, D), buf(NY, TOK, D), buf(NY, TOK, D)]
    outs = pl.pallas_call(
        kernel,
        out_shape=[jax.ShapeDtypeStruct((TOK, D), F32)] * 3
        + [jax.ShapeDtypeStruct((8, D), F32)] * 3,
        in_specs=[vmem] * 4 + [hbm] * 3 + [vmem] * 2,
        out_specs=[vmem] * 6,
        scratch_shapes=[buf(8, 2, TOK, D, dtype=BF16)] * 4
        + [
            buf(256, 64, dtype=BF16),
            buf(256, 128, dtype=BF16),
            buf(NY, 256, 1024, dtype=BF16),
            buf(NX, 256, 1024, dtype=BF16),
            buf(NZ, 8, D), buf(NZ, 8, D), buf(D, 128), buf(NZ, 8, D),
        ]
        + [buf(FS, 8 * TOK)] * 3
        + exchange
        + exchange
        + [
            buf(NZ, 16, D), buf(NZ, 16, D),
            buf(NZ, 8, 8, 128), buf(NZ, 8, 8, 128), buf(8, 8, 128), buf(8, 8, 128),
        ]
        + grads * 3
        + [pltpu.SemaphoreType.DMA((320,)), pltpu.SemaphoreType.DMA((3,))],
        compiler_params=pltpu.CompilerParams(
            collective_id=0, has_side_effects=True, vmem_limit_bytes=58 * 2**20
        ),
    )(
        queries, keys, values, rates,
        gate_fast.reshape(NY, NZ, 2, 8, D), up_fast.reshape(NY, NZ, 2, 8, D),
        down_fast.reshape(D, D), out_proj, out_grad,
    )
    return (*outs[:3], *(o.reshape(1, 8, D) for o in outs[3:]))


def solution(mesh):
    torus = Mesh(mesh.devices.reshape(NY, NZ, NC, NX), ("y", "z", "c", "head"))
    return jax.shard_map(
        body,
        mesh=torus,
        in_specs=(
            P(SEQ, "head"), P(SEQ, "head"), P(SEQ, "head"), P("head", SEQ),
            P("head", None, None), P("head", None, None), P("head", None, None),
            P("head", SEQ), P(SEQ, "head"),
        ),
        out_specs=(
            P(SEQ, "head"), P(SEQ, "head"), P(SEQ, "head"),
            P("head", SEQ, None), P("head", SEQ, None), P("head", SEQ, None),
        ),
        check_vma=False,
    )
```

profile of v0, /device:TPU:1, one launch (start us, length us, event | category | flops | bytes accessed | tf_op | source)
XLA Modules:
  0.0 156.7 jit_solution(18098553797869637201)
XLA Ops:
  0.6 1.6 %copy.15.oproj_ref = bf16[512,64]{1,0:T(8,128)(2,1)} copy(bf16[512,64]{0,1:T(8,128)(2,1)} %param.16) | data formatting | bytes 131072 | tf_op args[7]
  2.2 148.9 %shard_map.136 = (f32[128,512]{1,0:T(8,128)}, f32[128,512]{1,0:T(8,128)}, f32[128,512]{1,0:T(8,128)}, f32[8,512]{1,0:T(8,128)}, f32[8,512]{1,0:T(8,128)}, /*index=5*/f32[8,512]{1,0:T(8,128)}) custom-call(f32[128,512]{1,0:T(8,128)} %q_ref.1, f32[128,512]{1,0:T(8,128)} %k_ref.1, f32[128,512]{1,0:T(8,128)} %v_ref.1, f32[1,128]{1,0:T(1,128)} %rate_ref.1, ...), custom_call_target="tpu_custom_call" | custom-call | tf_op jit(solution)/shard_map/pallas_call | solution.py:471
  151.1 0.0 copy-start.1
  151.1 1.7 %copy.22 = f32[128,512]{1,0:T(8,128)} copy(f32[128,512]{1,0:T(8,128)} %get-tuple-element.24) | data formatting | bytes 524288
  152.9 0.0 copy-done.1
  152.9 0.0 copy-start
  152.9 0.7 copy.23
  153.6 0.3 copy-done
  153.9 0.0 copy-start.4
  153.9 0.7 copy.24
  154.6 0.0 copy-done.4
  154.6 0.0 copy-start.3
  154.6 0.6 copy.25
  155.2 0.1 copy-done.3
  155.3 0.0 copy-start.2
  155.4 0.6 copy.26
  156.0 0.1 copy-done.2
  156.1 0.6 copy.27
Async XLA Ops:
  151.1 1.7 %copy-start.1 = (f32[128,512]{1,0:T(8,128)S(1)}, f32[128,512]{1,0:T(8,128)}, u32[]{:S(2)}) copy-start(f32[128,512]{1,0:T(8,128)} %get-tuple-element.25) | copy-start | bytes 786436
  152.9 1.0 copy-start
  153.9 0.7 copy-start.4
  154.6 0.7 copy-start.3
  155.3 0.7 copy-start.2
where the time goes:
time: 157 us
  Pallas kernels  149 us (95%)
  local copies, waits for them, and re-layouts  7.13 us (5%)
    pallas_call x1, Pallas kernels, body(): pl.pallas_call(kernel, out_shape=[jax.ShapeDtypeStruct((TOK, D), F32)] *...  149 us
    unnamed x17, local copies, waits for them, and re-layouts  7.13 us

commit v1 on v0

v1 whole, which is shorter than its diff:
```python
import math

import jax
import jax.numpy as jnp
from jax import lax
from jax.experimental import pallas as pl
from jax.experimental.pallas import tpu as pltpu
from jax.sharding import Mesh
from jax.sharding import PartitionSpec as P

MESH = pl.DeviceIdType.MESH
SEQ = ("y", "z", "c")
F32 = jnp.float32
BF16 = jnp.bfloat16
NY, NZ, NC, NX = 4, 8, 2, 4
TOK = 128
D = 512
FS = 64
SCALE = 0.3 * math.sqrt(512)
EPS = 1e-06
SPAN = 251.0
LOW = 125.0


def halves(x):
    hi = x.astype(BF16)
    return hi, (x - hi.astype(F32)).astype(BF16)


def dot_nt(a, b):
    return lax.dot_general(a, b, (((1,), (1,)), ((), ())), preferred_element_type=F32)


def dot_nn(a, b):
    return lax.dot_general(a, b, (((1,), (0,)), ((), ())), preferred_element_type=F32)


def dot_tn(a, b):
    return lax.dot_general(a, b, (((0,), (0,)), ((), ())), preferred_element_type=F32)


def three(product, a, b_hi, b_lo):
    hi, lo = halves(a)
    n = a.shape[0]
    both = product(jnp.concatenate([hi, lo], axis=0), b_hi)
    return both[:n] + both[n:] + product(hi, b_lo)


def back(acts, mats):
    a_hi, a_lo = halves(acts)
    m_hi, m_lo = halves(mats)
    return dot_tn(
        jnp.concatenate([a_hi, a_lo, a_hi], axis=0), jnp.concatenate([m_hi, m_hi, m_lo], axis=0)
    )


def encode(x, top):
    size = jnp.exp2(jnp.abs(x) * (SPAN / top) - LOW)
    return jnp.where(x < 0, -size, size).astype(BF16)


def decode(codes):
    value = codes.astype(F32)
    size = jnp.log2(jnp.abs(value)) + LOW
    return jnp.where(value < 0, -size, size)


def row_top(x):
    return jnp.maximum(jnp.max(jnp.abs(x), axis=-1, keepdims=True), 1e-30)


def as_row(column):
    return jnp.broadcast_to(column, (TOK, TOK)).T[0:1]


def as_columns(row, tiles):
    return jnp.concatenate([jnp.broadcast_to(row, (TOK, TOK)).T] * tiles, axis=1)


def pack(gate, up, down):
    wide = jnp.concatenate([gate, up], axis=1)
    thin = jnp.concatenate([down[..., :256], down[..., 256:]], axis=1)
    top_w = (row_top(wide) * 1.01).astype(BF16)
    top_t = (row_top(thin) * 1.01).astype(BF16)
    top_w32, top_t32 = top_w.astype(F32), top_t.astype(F32)
    lanes = (*wide.shape[:2], 64)
    tops = jnp.concatenate(
        [jnp.broadcast_to(top_w32, lanes), jnp.broadcast_to(top_t32, lanes)], axis=2
    ).astype(BF16)
    return encode(wide, top_w32), encode(thin, top_t32), tops


def unpack(codes):
    tops = codes[..., 768:896].astype(F32) * (1.0 / SPAN)
    wide = decode(codes[..., :512]) * tops[..., 0:1]
    thin = decode(codes[..., 512:768]) * tops[..., 64:65]
    down = jnp.concatenate([thin[:, :8], thin[:, 8:]], axis=2)
    return wide[:, :8], wide[:, 8:], down


def row_sum(x):
    return jnp.sum(x, axis=1, keepdims=True)


def col_sum(x):
    return jnp.sum(x, axis=0, keepdims=True)


def total(x):
    return jnp.sum(jnp.sum(x, axis=1, keepdims=True), axis=0, keepdims=True)


def kernel(
    q_ref, k_ref, v_ref, rate_ref, g_hbm, u_hbm, w_hbm, oproj_ref, ograd_ref,
    qg_ref, kg_ref, vg_ref, gg_ref, ug_ref, dg_ref,
    k2, t2, q2, o2, kc, tc, qc, oc, tops_s, tops, otops, oproj_sib, oall, grads,
    gs, us, wcol, wts,
    before_s, linear_s, hgrad_s,
    s1, c1, r1, a1, st1, sty1, sts1, stz1,
    s2, c2, r2, a2, st2, sty2, sts2, stz2,
    s3, c3, r3, d3, rd3, ds3, dr3,
    part_q, sib_q, sum_q, code_q, ctop_q, rec_q, rtop_q,
    part_k, sib_k, sum_k, code_k, ctop_k, rec_k, rtop_k,
    part_t, sib_t, sum_t, code_t, ctop_t, rec_t, rtop_t,
    sems, lsem,
):
    y, z, c, x = (lax.axis_index(name) for name in ("y", "z", "c", "head"))
    used = [0]

    def at_y(dy, other=False):
        return (lax.rem(y + dy, NY), z, 1 - c if other else c, x)

    def at_z(dz):
        return (y, lax.rem(z + dz, NZ), c, x)

    def at_x(dx):
        return (y, z, c, lax.rem(x + dx, NX))

    sibling = (y, z, 1 - c, x)
    y_order = (1, 3, 2)
    z_order = (4, 3, 5, 2, 6, 1, 7)

    def send(src, dst, device):
        i = used[0]
        used[0] += 2
        copy = pltpu.make_async_remote_copy(
            src_ref=src, dst_ref=dst, send_sem=sems.at[i], recv_sem=sems.at[i + 1],
            device_id=device, device_id_type=MESH,
        )
        copy.start()
        started.append(copy)
        return copy

    started = []

    def arrived(copies):
        for copy in copies:
            copy.wait_recv()

    loads = []
    for i, (src, dst) in enumerate(
        (
            (g_hbm.at[y, :, c], gs),
            (u_hbm.at[y, :, c], us),
            (w_hbm.at[:, pl.ds(pl.multiple_of(y * 128, 128), 128)], wcol),
        )
    ):
        copy = pltpu.make_async_copy(src, dst, lsem.at[i])
        copy.start()
        loads.append(copy)

    barrier = pltpu.get_barrier_semaphore()
    partners = [sibling]
    partners += [at_y(d) for d in (1, 2, 3)] + [at_y(d, True) for d in (1, 2, 3)]
    partners += [at_z(d) for d in range(1, NZ)] + [at_x(d) for d in (1, 2, 3)]
    for device in partners:
        pl.semaphore_signal(barrier, inc=1, device_id=device, device_id_type=MESH)
    me = 2 * y + c
    first = c == 0
    rate_full = as_columns(rate_ref[...], 4)
    target = -(rate_full * v_ref[...])
    own_tops = []
    for buffer, codes, value in ((k2, kc, k_ref[...]), (t2, tc, target), (q2, qc, q_ref[...])):
        top = row_top(value)
        codes[me] = encode(value, top)
        own_tops.append(as_row(top * (1.0 / SPAN)))
        hi, lo = halves(value)
        buffer[me, 0] = hi
        buffer[me, 1] = lo
    tops_s[...] = jnp.concatenate(own_tops + [jnp.zeros((5, TOK), F32)], axis=0)
    tops[me] = jnp.ones((8, TOK), F32)
    tokens = pl.ds(pl.multiple_of(c * TOK, TOK), TOK)
    grads[x, tokens, :] = ograd_ref[...]

    pl.semaphore_wait(barrier, len(partners))

    osib = send(
        oproj_ref.at[:, pl.ds(pl.multiple_of((1 - c) * 256, 256), 256)], oproj_sib, sibling
    )
    xs = [send(grads.at[x, tokens], grads.at[x, tokens], at_x(d)) for d in (1, 3, 2)]
    gsib = [send(grads.at[x, tokens], grads.at[x, tokens], sibling)]
    tsends = [send(tops_s, tops.at[me], sibling)]
    tsends += [send(tops_s, tops.at[me], at_y(d)) for d in (1, 2, 3)]
    tsends += [send(tops_s, tops.at[me], at_y(d, True)) for d in (1, 2, 3)]

    def to_y(codes):
        return [send(codes.at[me], codes.at[me], at_y(d)) for d in y_order]

    def forward(codes, copies):
        result = []
        for d, copy in zip(y_order, copies):
            copy.wait_recv()
            block = 2 * lax.rem(y + NY - d, NY) + c
            result.append(send(codes.at[block], codes.at[block], sibling))
        return result

    def open_blocks(buffer, codes, core):
        for d in (1, 2, 3, 0) if core is not c else (1, 2, 3):
            block = 2 * lax.rem(y + d, NY) + core
            hi, lo = halves(decode(codes[block]))
            buffer[block, 0] = hi
            buffer[block, 1] = lo

    osib.wait_recv()
    own = oproj_ref[:, pl.ds(pl.multiple_of(c * 256, 256), 256)]
    yrows = pl.multiple_of(y * 128, 128)
    oall[z, pl.ds(pl.multiple_of(yrows + c * 64, 64), 64)] = own
    oall[z, pl.ds(pl.multiple_of(yrows + (1 - c) * 64, 64), 64)] = oproj_sib[...]
    ohere = oall.at[z, pl.ds(yrows, 128)]
    oy = [send(ohere, ohere, at_y(d)) for d in y_order]
    ky = to_y(kc)
    ty = to_y(tc)
    ksib = [send(kc.at[me], kc.at[me], sibling)]
    tsib = [send(tc.at[me], tc.at[me], sibling)]

    for copy in loads:
        copy.wait()
    wt = wcol[...].T.reshape(NZ, 2, 8, D)
    wts[...] = jnp.where(first, wt[:, 0], wt[:, 1])

    def ring(step, previous):
        result = {}
        for half in (0, 1):
            for way in (1, -1):
                if step == 4 and (half == 0) != (way == 1):
                    continue
                if previous is not None:
                    previous[half, way].wait_recv()
                block = lax.rem(z + NZ - way * (step - 1), NZ)
                part = oall.at[block, pl.ds(256 * half, 256)]
                result[half, way] = send(part, part, at_z((way + NZ) % NZ))
        if step == 4:
            for key in ((1, 1), (0, -1)):
                previous[key].wait_recv()
        return result

    arrived(oy)
    r1st = ring(1, None)
    r2nd = ring(2, r1st)
    ksib += forward(kc, ky)
    tsib += forward(tc, ty)
    qy = to_y(qc)
    qsib = [send(qc.at[me], qc.at[me], sibling)]
    open_blocks(k2, kc, c)
    open_blocks(t2, tc, c)
    r3rd = ring(3, r2nd)
    arrived(ksib)
    open_blocks(k2, kc, 1 - c)
    arrived(tsib)
    open_blocks(t2, tc, 1 - c)
    arrived(tsends)

    def scale_row(i):
        return jnp.concatenate([tops[b, i : i + 1] for b in range(8)], axis=1)

    k_scale, t_scale = scale_row(0), scale_row(1)

    def flat(ref):
        return ref[...].reshape(FS, D)

    def whole(buffer):
        return tuple(buffer[:, i].reshape(8 * TOK, D) for i in (0, 1))

    def silu_parts(before):
        sigma = jax.nn.sigmoid(before)
        return sigma, before * sigma, sigma * (1.0 + before * (1.0 - sigma))

    with jax.named_scope("partials"):
        both = k_scale * three(
            dot_nt, jnp.concatenate([flat(gs), flat(us)], axis=0), *whole(k2)
        )
        before, linear = both[:FS], both[FS:]
        hgrad = t_scale * three(dot_nt, flat(wts), *whole(t2))
        before_s[...] = before
        linear_s[...] = linear
        hgrad_s[...] = hgrad
        sigma, act, dsilu = silu_parts(before)
        pgu = three(
            dot_nn,
            k_scale * jnp.concatenate([hgrad * linear * dsilu, hgrad * act], axis=0),
            *whole(k2),
        )
        pd = three(dot_nn, t_scale * (act * linear), *whole(t2))

    def fill(plain, codes, gu, down):
        parts = [v.reshape(NZ, 8, D) for v in (gu[:FS], gu[FS:], down)]
        for i in range(3):
            plain[i] = parts[i]
        wide, thin, scales = pack(*parts)
        codes[:, :, 0:512] = wide
        codes[:, :, 512:768] = thin
        codes[:, :, 768:896] = scales

    def scatter_z(src, dst):
        return [
            send(src.at[lax.rem(z + d, NZ)], dst.at[z], at_z(d)) for d in z_order
        ]

    def summed(plain, dst, copies):
        value = [plain[i, z] for i in range(3)]
        for d, copy in zip(z_order, copies):
            copy.wait_recv()
            more = unpack(dst[pl.ds(lax.rem(z + NZ - d, NZ), 1)])
            value = [a + b[0] for a, b in zip(value, more)]
        return value

    def gather_z(codes, value):
        wide, thin, scales = pack(*(v[None] for v in value))
        codes[z, :, 0:512] = wide[0]
        codes[z, :, 512:768] = thin[0]
        codes[z, :, 768:896] = scales[0]
        return [send(codes.at[z], codes.at[z], at_z(d)) for d in z_order]

    def fold(row):
        return row[:, 0:128] + row[:, 128:256] + row[:, 256:384] + row[:, 384:512]

    def cut(row):
        return [row[:, 128 * i : 128 * (i + 1)] for i in range(4)]

    def uncut(stats, at):
        return jnp.concatenate([stats[at + i : at + i + 1] for i in range(4)], axis=1)

    def plane_start(st, sty, rows):
        value = jnp.concatenate(rows + [jnp.zeros((16 - len(rows), 128), F32)], axis=0)
        st[...] = value
        sty[me] = value
        sends = [send(st, sty.at[me], at_y(d)) for d in (2, 1, 3)]
        sends += [send(st, sty.at[me], at_y(d, True)) for d in (2, 1, 3)]
        return sends + [send(st, sty.at[me], sibling)]

    def plane_finish(sends, sty, sts, stz):
        arrived(sends)
        group = jnp.sum(sty[...], axis=0)
        sts[...] = group
        stz[z] = group
        return [send(sts, stz.at[z], at_z(d)) for d in z_order]

    fill(s1, c1, pgu, pd)
    rs1 = scatter_z(c1, r1)

    for d, copy in zip((1, 3, 2), xs):
        copy.wait_recv()
        src = lax.rem(x + NX - d, NX)
        gsib.append(send(grads.at[src, tokens], grads.at[src, tokens], sibling))
    r4th = ring(4, r3rd)
    qsib += forward(qc, qy)
    open_blocks(q2, qc, c)

    pg_c, pu_c, pd_c = summed(s1, r1, rs1)
    ag1 = gather_z(a1, (pg_c, pu_c, pd_c))
    gc, uc, wc = gs[z], us[z], wts[z]
    ys1 = plane_start(
        st1, sty1,
        [fold(col_sum(pg_c * pg_c)), fold(col_sum(pu_c * pu_c))]
        + cut(col_sum(pd_c * pd_c)) + cut(col_sum(wc * pd_c)) + cut(col_sum(wc * wc)),
    )

    arrived(gsib)
    arrived(r4th.values())
    cot = jnp.zeros((256, 256), F32)
    for i in range(NZ):
        both = jnp.concatenate(
            [grads[j, :, 128 * i : 128 * (i + 1)] for j in range(NX)], axis=1
        )
        cot = cot + dot_nn(both, oall[i])
    rows = pl.ds(2 * y, 2)

    def half(core):
        return pl.ds(pl.multiple_of(core * 256, 256), 256)

    cot_top = row_top(cot)
    oc[rows, :, half(c)] = encode(cot, cot_top).reshape(2, TOK, 256)
    for j in (0, 1):
        otops[c, 2 * y + j] = jnp.broadcast_to(
            as_row(cot_top[TOK * j : TOK * (j + 1)] * (1.0 / SPAN)), (8, TOK)
        )
    tops_here = otops.at[c, rows]
    here = oc.at[rows, :, half(c)]
    otsends = [send(tops_here, tops_here, at_y(d)) for d in y_order]
    otsends += [send(tops_here, tops_here, at_y(d, True)) for d in y_order]
    otsends += [send(tops_here, tops_here, sibling)]
    coty = [send(here, here, at_y(d)) for d in y_order]
    cotsib = [send(here, here, sibling)]
    cot_hi, cot_lo = halves(cot)
    o2[rows, 0, :, half(c)] = cot_hi.reshape(2, TOK, 256)
    o2[rows, 1, :, half(c)] = cot_lo.reshape(2, TOK, 256)

    zs1 = plane_finish(ys1, sty1, sts1, stz1)

    arrived(qsib)
    open_blocks(q2, qc, 1 - c)
    q_scale = scale_row(2)
    for d, copy in zip(y_order, coty):
        copy.wait_recv()
        there = oc.at[pl.ds(2 * lax.rem(y + NY - d, NY), 2), :, half(c)]
        cotsib.append(send(there, there, sibling))

    def open_cot(core):
        for d in (1, 2, 3, 0) if core is not c else (1, 2, 3):
            for j in (0, 1):
                block = 2 * lax.rem(y + d, NY) + j
                scale = as_columns(otops[core, block][0:1], 2)
                hi, lo = halves(decode(oc[block, :, half(core)]) * scale)
                o2[block, 0, :, half(core)] = hi
                o2[block, 1, :, half(core)] = lo

    arrived(otsends)
    open_cot(c)
    arrived(cotsib)
    open_cot(1 - c)
    arrived(zs1)
    arrived(ag1)

    with jax.named_scope("renormed"):
        stats = jnp.sum(stz1[...], axis=0)
        d_pp, d_wp, d_ww = uncut(stats, 2), uncut(stats, 6), uncut(stats, 10)
        pn_g = jnp.sqrt(total(stats[0:1]) + EPS)
        pn_u = jnp.sqrt(total(stats[1:2]) + EPS)
        pn_d = jnp.sqrt(total(d_pp) + EPS)
        k_g, k_u, k_d = SCALE / pn_g, SCALE / pn_u, SCALE / pn_d
        old_d = jnp.sqrt(d_ww + EPS)
        new_d = jnp.sqrt(
            jnp.maximum(d_ww - 2.0 * k_d * d_wp + k_d * k_d * d_pp, 0.0) + EPS
        )
        d_pm = d_wp - k_d * d_pp

        def moved_rows(matrix, partial, k):
            moved = matrix - partial * k
            old = jnp.sqrt(row_sum(matrix * matrix) + EPS)
            new = jnp.sqrt(row_sum(moved * moved) + EPS)
            return moved, old, new

        g_m, u_m, w_m = flat(gs), flat(us), flat(wts)
        p_g, p_u, p_d = (v.reshape(FS, D) for v in unpack(a1[...]))
        mv_g, old_g, new_g = moved_rows(g_m, p_g, k_g)
        mv_u, old_u, new_u = moved_rows(u_m, p_u, k_u)
        mv_d = w_m - p_d * k_d
        ren_gu = jnp.concatenate([mv_g * (old_g / new_g), mv_u * (old_u / new_u)], axis=0)
        ren_d = mv_d * (old_d / new_d)

    with jax.named_scope("cotangents"):
        both = q_scale * three(dot_nt, ren_gu, *whole(q2))
        before, linear = both[:FS], both[FS:]
        hcot = three(dot_nt, ren_d, *whole(o2))
        sigma, act, dsilu = silu_parts(before)
        acts_q = jnp.concatenate([hcot * linear * dsilu, hcot * act], axis=0)
        cgu = three(dot_nn, q_scale * acts_q, *whole(q2))
        cd = three(dot_nn, act * linear, *whole(o2))
        fill(s2, c2, cgu, cd)
    rs2 = scatter_z(c2, r2)
    with jax.named_scope("query_grad"):
        part_q[...] = back(acts_q, ren_gu).reshape(NY, 2, TOK, D)
    sibq = send(part_q.at[:, 1 - c], sib_q, sibling)

    cg_c, cu_c, cd_c = summed(s2, r2, rs2)
    ag2 = gather_z(a2, (cg_c, cu_c, cd_c))

    def row_back(matrix, partial, k, grad):
        moved, old, new = moved_rows(matrix, partial, k)
        along = row_sum(moved * grad)
        moved_grad = (old / new) * (grad - moved * (along / (new * new)))
        return moved_grad, moved_grad + (along / (new * old)) * matrix

    mg_c, direct_g = row_back(gc, pg_c, k_g, cg_c)
    mu_c, direct_u = row_back(uc, pu_c, k_u, cu_c)
    ys2 = plane_start(
        st2, sty2,
        [fold(-col_sum(pg_c * mg_c)), fold(-col_sum(pu_c * mu_c))]
        + cut(col_sum((wc - pd_c * k_d) * cd_c)) + cut(col_sum(pd_c * cd_c)),
    )

    def to_owner(part, sib, plain, codes, scales, rec, rec_scales, copy):
        copy.wait_recv()
        value = part[:, c] + sib[...]
        plain[...] = value
        top = row_top(value)
        codes[...] = encode(value, top)
        for i in range(NY):
            scales[i] = jnp.broadcast_to(as_row(top[i] * (1.0 / SPAN)), (8, TOK))
        sends = []
        for d in y_order:
            to = lax.rem(y + d, NY)
            sends.append(
                (
                    send(codes.at[to], rec.at[y], at_y(d)),
                    send(scales.at[to], rec_scales.at[y], at_y(d)),
                )
            )
        return sends

    def owned(plain, rec, rec_scales, copies):
        value = plain[y]
        for d, pair in zip(y_order, copies):
            arrived(pair)
            src = lax.rem(y + NY - d, NY)
            value = value + decode(rec[src]) * as_columns(rec_scales[src][0:1], 4)
        return value

    yq = to_owner(part_q, sib_q, sum_q, code_q, ctop_q, rec_q, rtop_q, sibq)
    zs2 = plane_finish(ys2, sty2, sts2, stz2)

    arrived(zs2)
    arrived(ag2)
    with jax.named_scope("direction"):
        stats2 = jnp.sum(stz2[...], axis=0)
        inner_g, inner_u = total(stats2[0:1]), total(stats2[1:2])
        along_d, d_pg = uncut(stats2, 2), uncut(stats2, 6)
        ratio_d = old_d / new_d
        shrink_d = along_d / (new_d * new_d)
        inner_d = -total(ratio_d * (d_pg - d_pm * shrink_d))
        c_g, c_u, c_d = (v.reshape(FS, D) for v in unpack(a2[...]))
        mgrad_g, _ = row_back(g_m, p_g, k_g, c_g)
        mgrad_u, _ = row_back(u_m, p_u, k_u, c_u)
        mgrad_d = ratio_d * (c_d - mv_d * shrink_d)
        direct_d = mgrad_d + (along_d / (new_d * old_d)) * w_m
        dir_g = -k_g * (mgrad_g + p_g * (inner_g / (pn_g * pn_g)))
        dir_u = -k_u * (mgrad_u + p_u * (inner_u / (pn_u * pn_u)))
        dir_d = -k_d * (mgrad_d + p_d * (inner_d / (pn_d * pn_d)))

    with jax.named_scope("through"):
        both = k_scale * three(dot_nt, jnp.concatenate([dir_g, dir_u], axis=0), *whole(k2))
        d_bg, d_lg = both[:FS], both[FS:]
        d_hid = t_scale * three(dot_nt, dir_d, *whole(t2))
        before, linear, hgrad = before_s[...], linear_s[...], hgrad_s[...]
        sigma, act, dsilu = silu_parts(before)
        curve = sigma * (1.0 - sigma) * (2.0 + before * (1.0 - 2.0 * sigma))
        d_h = d_bg * linear * dsilu + d_lg * act
        d_l = d_bg * hgrad * dsilu + d_hid * act
        d_b = d_bg * hgrad * linear * curve + (d_lg * hgrad + d_hid * linear) * dsilu
        part_t[...] = back(
            jnp.concatenate([act * linear, d_h], axis=0),
            jnp.concatenate([dir_d, w_m], axis=0),
        ).reshape(NY, 2, TOK, D)
        sibt = send(part_t.at[:, 1 - c], sib_t, sibling)
        part_k[...] = back(
            jnp.concatenate([hgrad * linear * dsilu, hgrad * act, d_b, d_l], axis=0),
            jnp.concatenate([dir_g, dir_u, g_m, u_m], axis=0),
        ).reshape(NY, 2, TOK, D)
        sibk = send(part_k.at[:, 1 - c], sib_k, sibling)
        yt = to_owner(part_t, sib_t, sum_t, code_t, ctop_t, rec_t, rtop_t, sibt)
        th_d = three(dot_nn, t_scale * d_h, *whole(t2))
        th_d = th_d + jnp.where(z == 0, direct_d, jnp.zeros_like(direct_d))
        th_d = th_d.reshape(NZ, 1, 8, D)
        none = jnp.zeros_like(th_d)
        th_d = jnp.concatenate(
            [jnp.where(first, th_d, none), jnp.where(first, none, th_d)], axis=1
        ).reshape(2 * FS, D)
        th_t = th_d.T.reshape(NY, NZ, 2, 8, 2 * FS)
        for i in range(NZ):
            d3[i] = th_t[:, i].reshape(8, 8, 2 * FS)
        rsd = scatter_z(d3, rd3)
        yk = to_owner(part_k, sib_k, sum_k, code_k, ctop_k, rec_k, rtop_k, sibk)
        th_gu = three(dot_nn, k_scale * jnp.concatenate([d_b, d_l], axis=0), *whole(k2))
        th_gu = jnp.concatenate(
            [th_gu[:FS].reshape(NZ, 8, D), th_gu[FS:].reshape(NZ, 8, D)], axis=1
        )
        s3[...] = th_gu
        top_bf = (row_top(th_gu) * 1.01).astype(BF16)
        top = top_bf.astype(F32)
        c3[:, :, 0:512] = encode(th_gu, top)
        c3[:, :, 512:640] = jnp.broadcast_to(top, (NZ, 16, 128)).astype(BF16)
        rs3 = scatter_z(c3, r3)

    qg_ref[...] = owned(sum_q, rec_q, rtop_q, yq)
    down = d3[z]
    for d, copy in zip(z_order, rsd):
        copy.wait_recv()
        down = down + rd3[lax.rem(z + NZ - d, NZ)]
    ds3[...] = down
    dr3[me] = ds3[me]
    fin = [send(ds3.at[2 * y + 1 - c], dr3.at[me], sibling)]
    for d in (1, 2, 3):
        to = 2 * lax.rem(y + d, NY)
        fin.append(send(ds3.at[to + c], dr3.at[me], at_y(d)))
        fin.append(send(ds3.at[to + 1 - c], dr3.at[me], at_y(d, True)))
    vg_ref[...] = -(rate_full * owned(sum_t, rec_t, rtop_t, yt))
    kg_ref[...] = owned(sum_k, rec_k, rtop_k, yk)
    gate_up = s3[z]
    for d, copy in zip(z_order, rs3):
        copy.wait_recv()
        codes = r3[lax.rem(z + NZ - d, NZ)]
        gate_up = gate_up + decode(codes[:, 0:512]) * (
            codes[:, 512:640].astype(F32)[:, 0:1] * (1.0 / SPAN)
        )
    gg_ref[...] = gate_up[0:8] + direct_g
    ug_ref[...] = gate_up[8:16] + direct_u
    arrived(fin)
    dg_ref[...] = jnp.concatenate(
        [dr3[2 * i] + dr3[2 * i + 1] for i in range(NY)], axis=1
    )
    for copy in started:
        copy.wait_send()


def hand_over(*refs):
    sems = refs[-1]
    copies = [pltpu.make_async_copy(refs[i], refs[6 + i], sems.at[i]) for i in range(6)]
    for copy in copies:
        copy.start()
    for copy in copies:
        copy.wait()


def body(queries, keys, values, rates, gate_fast, up_fast, down_fast, out_proj, out_grad):
    vmem = pl.BlockSpec(memory_space=pltpu.VMEM)
    hbm = pl.BlockSpec(memory_space=pl.ANY)

    def buf(*shape, dtype=F32):
        return pltpu.VMEM(shape, dtype)

    exchange = [
        buf(3, NZ, 8, D), *[buf(NZ, 16, 896, dtype=BF16)] * 3,
        buf(16, 128), buf(8, 16, 128), buf(16, 128), buf(NZ, 16, 128),
    ]
    grads = [
        buf(NY, 2, TOK, D), buf(NY, TOK, D), buf(NY, TOK, D),
        buf(NY, TOK, D, dtype=BF16), buf(NY, 8, TOK),
        buf(NY, TOK, D, dtype=BF16), buf(NY, 8, TOK),
    ]
    outs = pl.pallas_call(
        kernel,
        out_shape=[jax.ShapeDtypeStruct((TOK, D), F32)] * 3
        + [jax.ShapeDtypeStruct((8, D), F32)] * 3,
        in_specs=[vmem] * 4 + [hbm] * 3 + [vmem] * 2,
        out_specs=[vmem] * 6,
        scratch_shapes=[buf(8, 2, TOK, D, dtype=BF16)] * 4
        + [buf(8, TOK, D, dtype=BF16)] * 4
        + [
            buf(8, TOK), buf(8, 8, TOK), buf(2, 8, 8, TOK),
            buf(64, 256, dtype=BF16),
            buf(NZ, 512, 256, dtype=BF16),
            buf(NX, 256, 1024, dtype=BF16),
            buf(NZ, 8, D), buf(NZ, 8, D), buf(D, 128), buf(NZ, 8, D),
        ]
        + [buf(FS, 8 * TOK)] * 3
        + exchange
        + exchange
        + [
            buf(NZ, 16, D), *[buf(NZ, 16, 640, dtype=BF16)] * 2,
            buf(NZ, 8, 8, 128), buf(NZ, 8, 8, 128), buf(8, 8, 128), buf(8, 8, 128),
        ]
        + grads * 3
        + [pltpu.SemaphoreType.DMA((420,)), pltpu.SemaphoreType.DMA((3,))],
        compiler_params=pltpu.CompilerParams(
            collective_id=0, has_side_effects=True, vmem_limit_bytes=58 * 2**20
        ),
    )(
        queries, keys, values, rates,
        gate_fast.reshape(NY, NZ, 2, 8, D), up_fast.reshape(NY, NZ, 2, 8, D),
        down_fast.reshape(D, D), out_proj.T, out_grad,
    )
    outs = pl.pallas_call(
        hand_over,
        out_shape=[jax.ShapeDtypeStruct(o.shape, F32) for o in outs],
        in_specs=[hbm] * 6,
        out_specs=[hbm] * 6,
        scratch_shapes=[pltpu.SemaphoreType.DMA((6,))],
    )(*outs)
    return (*outs[:3], *(o.reshape(1, 8, D) for o in outs[3:]))


def solution(mesh):
    torus = Mesh(mesh.devices.reshape(NY, NZ, NC, NX), ("y", "z", "c", "head"))
    return jax.shard_map(
        body,
        mesh=torus,
        in_specs=(
            P(SEQ, "head"), P(SEQ, "head"), P(SEQ, "head"), P("head", SEQ),
            P("head", None, None), P("head", None, None), P("head", None, None),
            P("head", SEQ), P(SEQ, "head"),
        ),
        out_specs=(
            P(SEQ, "head"), P(SEQ, "head"), P(SEQ, "head"),
            P("head", SEQ, None), P("head", SEQ, None), P("head", SEQ, None),
        ),
        check_vma=False,
    )
```

time: 157 us -> 128 us (0.82)
  Pallas kernels: 149 us -> 127 us
  local copies, waits for them, and re-layouts: 7.13 us -> 0 us
    pallas_call x1, Pallas kernels: 149 us -> 101 us  [body(): pl.pallas_call(kernel, out_shape=[jax.ShapeDtypeStruct((TOK, D), F32)] *...]
    pallas_call x0 -> x1, Pallas kernels: none -> 26.5 us  [body(): pl.pallas_call(hand_over, out_shape=[jax.ShapeDtypeStruct(o.shape, F32) f...]
    unnamed x17 -> x0, local copies, waits for them, and re-layouts: 7.13 us -> none
where the time goes in v1:
time: 128 us
  Pallas kernels  127 us (99%)
    pallas_call x1, Pallas kernels, body(): pl.pallas_call(kernel, out_shape=[jax.ShapeDtypeStruct((TOK, D), F32)] *...  101 us
    pallas_call x1, Pallas kernels, body(): pl.pallas_call(hand_over, out_shape=[jax.ShapeDtypeStruct(o.shape, F32) f...  26.5 us

profile of v1, /device:TPU:1, one launch (start us, length us, event | category | flops | bytes accessed | tf_op | source)
XLA Modules:
  0.0 128.1 jit_solution(3692174549779964921)
XLA Ops:
  0.6 100.8 %shard_map.136 = (f32[128,512]{1,0:T(8,128)}, f32[128,512]{1,0:T(8,128)}, f32[128,512]{1,0:T(8,128)}, f32[8,512]{1,0:T(8,128)}, f32[8,512]{1,0:T(8,128)}, /*index=5*/f32[8,512]{1,0:T(8,128)}) custom-call(f32[128,512]{1,0:T(8,128)} %q_ref.1, f32[128,512]{1,0:T(8,128)} %k_ref.1, f32[128,512]{1,0:T(8,128)} %v_ref.1, f32[1,128]{1,0:T(1,128)} %rate_ref.1, ...), custom_call_target="tpu_custom_call" | custom-call | tf_op jit(solution)/shard_map/pallas_call | solution.py:640
  101.5 26.5 %shard_map.137 = (f32[128,512]{1,0:T(8,128)}, f32[128,512]{1,0:T(8,128)}, f32[128,512]{1,0:T(8,128)}, f32[8,512]{1,0:T(8,128)}, f32[8,512]{1,0:T(8,128)}, /*index=5*/f32[8,512]{1,0:T(8,128)}) custom-call(f32[128,512]{1,0:T(8,128)} %get-tuple-element.18.refs_0_, f32[128,512]{1,0:T(8,128)} %get-tuple-element.19.refs_1_, f32[128,512]{1,0:T(8,128)} %get-tuple-element.20.refs_2_, ...), custom_call_target="tpu_custom_call" | custom-call | tf_op jit(solution)/shard_map/pallas_call | solution.py:672

commit v2 on v1

--- a/solution.py
+++ b/solution.py
@@ -20,6 +20,8 @@
 EPS = 1e-06
 SPAN = 251.0
 LOW = 125.0
+LN2 = math.log(2.0)
+STEP = 1.0 / (SPAN * LN2)
 
 
 def halves(x):
@@ -55,13 +57,13 @@
 
 
 def encode(x, top):
-    size = jnp.exp2(jnp.abs(x) * (SPAN / top) - LOW)
+    size = jnp.exp(jnp.abs(x) * (SPAN * LN2 / top) - LOW * LN2)
     return jnp.where(x < 0, -size, size).astype(BF16)
 
 
 def decode(codes):
     value = codes.astype(F32)
-    size = jnp.log2(jnp.abs(value)) + LOW
+    size = jnp.log(jnp.abs(value)) + LOW * LN2
     return jnp.where(value < 0, -size, size)
 
 
@@ -91,7 +93,7 @@
 
 
 def unpack(codes):
-    tops = codes[..., 768:896].astype(F32) * (1.0 / SPAN)
+    tops = codes[..., 768:896].astype(F32) * STEP
     wide = decode(codes[..., :512]) * tops[..., 0:1]
     thin = decode(codes[..., 512:768]) * tops[..., 64:65]
     down = jnp.concatenate([thin[:, :8], thin[:, 8:]], axis=2)
@@ -113,10 +115,10 @@
 def kernel(
     q_ref, k_ref, v_ref, rate_ref, g_hbm, u_hbm, w_hbm, oproj_ref, ograd_ref,
     qg_ref, kg_ref, vg_ref, gg_ref, ug_ref, dg_ref,
-    k2, t2, q2, o2, kc, tc, qc, oc, tops_s, tops, otops, oproj_sib, oall, grads,
+    k1, t1, k2, t2, q2, o2, kc, tc, qc, oc, tops_s, tops, otops, oproj_sib, oall, grads,
     gs, us, wcol, wts,
     before_s, linear_s, hgrad_s,
-    s1, c1, r1, a1, st1, sty1, sts1, stz1,
+    p1, pc1, pr1, s1, c1, r1, a1, st1, sty1, sts1, stz1,
     s2, c2, r2, a2, st2, sty2, sts2, stz2,
     s3, c3, r3, d3, rd3, ds3, dr3,
     part_q, sib_q, sum_q, code_q, ctop_q, rec_q, rtop_q,
@@ -160,9 +162,9 @@
     loads = []
     for i, (src, dst) in enumerate(
         (
-            (g_hbm.at[y, :, c], gs),
-            (u_hbm.at[y, :, c], us),
-            (w_hbm.at[:, pl.ds(pl.multiple_of(y * 128, 128), 128)], wcol),
+            (g_hbm.at[:, :, c], gs),
+            (u_hbm.at[:, :, c], us),
+            (w_hbm, wcol),
         )
     ):
         copy = pltpu.make_async_copy(src, dst, lsem.at[i])
@@ -179,47 +181,36 @@
     first = c == 0
     rate_full = as_columns(rate_ref[...], 4)
     target = -(rate_full * v_ref[...])
-    own_tops = []
-    for buffer, codes, value in ((k2, kc, k_ref[...]), (t2, tc, target), (q2, qc, q_ref[...])):
-        top = row_top(value)
-        codes[me] = encode(value, top)
-        own_tops.append(as_row(top * (1.0 / SPAN)))
-        hi, lo = halves(value)
-        buffer[me, 0] = hi
-        buffer[me, 1] = lo
-    tops_s[...] = jnp.concatenate(own_tops + [jnp.zeros((5, TOK), F32)], axis=0)
-    tops[me] = jnp.ones((8, TOK), F32)
+    for near, value in ((k1, k_ref[...]), (t1, target)):
+        for i, part in enumerate(halves(value)):
+            near[c, i] = part
     tokens = pl.ds(pl.multiple_of(c * TOK, TOK), TOK)
     grads[x, tokens, :] = ograd_ref[...]
+    for copy in loads:
+        copy.wait()
+    wt = wcol[...].T.reshape(NY, NZ, 2, 8, D)
+    wts[...] = jnp.where(first, wt[:, :, 0], wt[:, :, 1])
 
     pl.semaphore_wait(barrier, len(partners))
 
     osib = send(
         oproj_ref.at[:, pl.ds(pl.multiple_of((1 - c) * 256, 256), 256)], oproj_sib, sibling
     )
+    near = [send(k1.at[c], k1.at[c], sibling), send(t1.at[c], t1.at[c], sibling)]
     xs = [send(grads.at[x, tokens], grads.at[x, tokens], at_x(d)) for d in (1, 3, 2)]
     gsib = [send(grads.at[x, tokens], grads.at[x, tokens], sibling)]
-    tsends = [send(tops_s, tops.at[me], sibling)]
-    tsends += [send(tops_s, tops.at[me], at_y(d)) for d in (1, 2, 3)]
-    tsends += [send(tops_s, tops.at[me], at_y(d, True)) for d in (1, 2, 3)]
-
     def to_y(codes):
-        return [send(codes.at[me], codes.at[me], at_y(d)) for d in y_order]
-
-    def forward(codes, copies):
+        return {d: send(codes.at[me], codes.at[me], at_y(d)) for d in y_order}
+
+    def open_blocks(buffer, codes, copies):
         result = []
-        for d, copy in zip(y_order, copies):
-            copy.wait_recv()
+        for d in y_order:
+            copies[d].wait_recv()
             block = 2 * lax.rem(y + NY - d, NY) + c
-            result.append(send(codes.at[block], codes.at[block], sibling))
+            for i, part in enumerate(halves(decode(codes[block]))):
+                buffer[block, i] = part
+            result.append(send(buffer.at[block], buffer.at[block], sibling))
         return result
-
-    def open_blocks(buffer, codes, core):
-        for d in (1, 2, 3, 0) if core is not c else (1, 2, 3):
-            block = 2 * lax.rem(y + d, NY) + core
-            hi, lo = halves(decode(codes[block]))
-            buffer[block, 0] = hi
-            buffer[block, 1] = lo
 
     osib.wait_recv()
     own = oproj_ref[:, pl.ds(pl.multiple_of(c * 256, 256), 256)]
@@ -228,16 +219,6 @@
     oall[z, pl.ds(pl.multiple_of(yrows + (1 - c) * 64, 64), 64)] = oproj_sib[...]
     ohere = oall.at[z, pl.ds(yrows, 128)]
     oy = [send(ohere, ohere, at_y(d)) for d in y_order]
-    ky = to_y(kc)
-    ty = to_y(tc)
-    ksib = [send(kc.at[me], kc.at[me], sibling)]
-    tsib = [send(tc.at[me], tc.at[me], sibling)]
-
-    for copy in loads:
-        copy.wait()
-    wt = wcol[...].T.reshape(NZ, 2, 8, D)
-    wts[...] = jnp.where(first, wt[:, 0], wt[:, 1])
-
     def ring(step, previous):
         result = {}
         for half in (0, 1):
@@ -254,29 +235,11 @@
                 previous[key].wait_recv()
         return result
 
-    arrived(oy)
-    r1st = ring(1, None)
-    r2nd = ring(2, r1st)
-    ksib += forward(kc, ky)
-    tsib += forward(tc, ty)
-    qy = to_y(qc)
-    qsib = [send(qc.at[me], qc.at[me], sibling)]
-    open_blocks(k2, kc, c)
-    open_blocks(t2, tc, c)
-    r3rd = ring(3, r2nd)
-    arrived(ksib)
-    open_blocks(k2, kc, 1 - c)
-    arrived(tsib)
-    open_blocks(t2, tc, 1 - c)
-    arrived(tsends)
-
     def scale_row(i):
         return jnp.concatenate([tops[b, i : i + 1] for b in range(8)], axis=1)
 
-    k_scale, t_scale = scale_row(0), scale_row(1)
-
     def flat(ref):
-        return ref[...].reshape(FS, D)
+        return ref[y].reshape(FS, D)
 
     def whole(buffer):
         return tuple(buffer[:, i].reshape(8 * TOK, D) for i in (0, 1))
@@ -285,25 +248,61 @@
         sigma = jax.nn.sigmoid(before)
         return sigma, before * sigma, sigma * (1.0 + before * (1.0 - sigma))
 
+    arrived(near)
     with jax.named_scope("partials"):
-        both = k_scale * three(
-            dot_nt, jnp.concatenate([flat(gs), flat(us)], axis=0), *whole(k2)
-        )
-        before, linear = both[:FS], both[FS:]
-        hgrad = t_scale * three(dot_nt, flat(wts), *whole(t2))
-        before_s[...] = before
-        linear_s[...] = linear
-        hgrad_s[...] = hgrad
+        k_near = tuple(k1[:, i].reshape(2 * TOK, D) for i in (0, 1))
+        t_near = tuple(t1[:, i].reshape(2 * TOK, D) for i in (0, 1))
+        n = NY * FS
+        both = three(
+            dot_nt,
+            jnp.concatenate([gs[...].reshape(n, D), us[...].reshape(n, D)], axis=0),
+            *k_near,
+        )
+        before, linear = both[:n], both[n:]
+        hgrad = three(dot_nt, wts[...].reshape(n, D), *t_near)
+    arrived(oy)
+    r1st = ring(1, None)
+    with jax.named_scope("partials"):
         sigma, act, dsilu = silu_parts(before)
         pgu = three(
-            dot_nn,
-            k_scale * jnp.concatenate([hgrad * linear * dsilu, hgrad * act], axis=0),
-            *whole(k2),
-        )
-        pd = three(dot_nn, t_scale * (act * linear), *whole(t2))
-
-    def fill(plain, codes, gu, down):
-        parts = [v.reshape(NZ, 8, D) for v in (gu[:FS], gu[FS:], down)]
+            dot_nn, jnp.concatenate([hgrad * linear * dsilu, hgrad * act], axis=0), *k_near
+        )
+        p1[0] = pgu[:n].reshape(NY, NZ, 8, D)
+        p1[1] = pgu[n:].reshape(NY, NZ, 8, D)
+        p1[2] = three(dot_nn, act * linear, *t_near).reshape(NY, NZ, 8, D)
+
+    def put(codes, index, values):
+        wide, thin, scales = pack(*values)
+        codes[index, :, :, 0:512] = wide
+        codes[index, :, :, 512:768] = thin
+        codes[index, :, :, 768:896] = scales
+
+    py = {}
+    for d in (2, 1, 3):
+        to = lax.rem(y + d, NY)
+        put(pc1, to, tuple(p1[i, to] for i in range(3)))
+        py[d] = send(pc1.at[to], pr1.at[y], at_y(d))
+    r2nd = ring(2, r1st)
+
+    own_tops = []
+    for buffer, near, codes, value in (
+        (k2, k1, kc, k_ref[...]), (t2, t1, tc, target), (q2, None, qc, q_ref[...])
+    ):
+        top = row_top(value)
+        codes[me] = encode(value, top)
+        own_tops.append(as_row(top * STEP))
+        if near is None:
+            for i, part in enumerate(halves(value)):
+                buffer[me, i] = part
+        else:
+            buffer[pl.ds(2 * y, 2)] = near[...]
+    tops_s[...] = jnp.concatenate(own_tops + [jnp.zeros((5, TOK), F32)], axis=0)
+    tops[pl.ds(2 * y, 2)] = jnp.ones((2, 8, TOK), F32)
+    tsends = [send(tops_s, tops.at[me], at_y(d)) for d in (1, 2, 3)]
+    tsends += [send(tops_s, tops.at[me], at_y(d, True)) for d in (1, 2, 3)]
+    qsib = [send(q2.at[me], q2.at[me], sibling)]
+
+    def fill(plain, codes, parts):
         for i in range(3):
             plain[i] = parts[i]
         wide, thin, scales = pack(*parts)
@@ -355,26 +354,21 @@
         stz[z] = group
         return [send(sts, stz.at[z], at_z(d)) for d in z_order]
 
-    fill(s1, c1, pgu, pd)
+    r3rd = ring(3, r2nd)
+    r4th = ring(4, r3rd)
+    mine = [p1[i, y] for i in range(3)]
+    for d in (1, 3, 2):
+        py[d].wait_recv()
+        more = unpack(pr1[lax.rem(y + NY - d, NY)])
+        mine = [a + b for a, b in zip(mine, more)]
+    fill(s1, c1, mine)
     rs1 = scatter_z(c1, r1)
+    qy = to_y(qc)
 
     for d, copy in zip((1, 3, 2), xs):
         copy.wait_recv()
         src = lax.rem(x + NX - d, NX)
         gsib.append(send(grads.at[src, tokens], grads.at[src, tokens], sibling))
-    r4th = ring(4, r3rd)
-    qsib += forward(qc, qy)
-    open_blocks(q2, qc, c)
-
-    pg_c, pu_c, pd_c = summed(s1, r1, rs1)
-    ag1 = gather_z(a1, (pg_c, pu_c, pd_c))
-    gc, uc, wc = gs[z], us[z], wts[z]
-    ys1 = plane_start(
-        st1, sty1,
-        [fold(col_sum(pg_c * pg_c)), fold(col_sum(pu_c * pu_c))]
-        + cut(col_sum(pd_c * pd_c)) + cut(col_sum(wc * pd_c)) + cut(col_sum(wc * wc)),
-    )
-
     arrived(gsib)
     arrived(r4th.values())
     cot = jnp.zeros((256, 256), F32)
@@ -392,42 +386,47 @@
     oc[rows, :, half(c)] = encode(cot, cot_top).reshape(2, TOK, 256)
     for j in (0, 1):
         otops[c, 2 * y + j] = jnp.broadcast_to(
-            as_row(cot_top[TOK * j : TOK * (j + 1)] * (1.0 / SPAN)), (8, TOK)
+            as_row(cot_top[TOK * j : TOK * (j + 1)] * STEP), (8, TOK)
         )
     tops_here = otops.at[c, rows]
     here = oc.at[rows, :, half(c)]
     otsends = [send(tops_here, tops_here, at_y(d)) for d in y_order]
-    otsends += [send(tops_here, tops_here, at_y(d, True)) for d in y_order]
-    otsends += [send(tops_here, tops_here, sibling)]
-    coty = [send(here, here, at_y(d)) for d in y_order]
-    cotsib = [send(here, here, sibling)]
+    coty = {d: send(here, here, at_y(d)) for d in y_order}
     cot_hi, cot_lo = halves(cot)
     o2[rows, 0, :, half(c)] = cot_hi.reshape(2, TOK, 256)
     o2[rows, 1, :, half(c)] = cot_lo.reshape(2, TOK, 256)
+    there = o2.at[rows, :, :, half(c)]
+    cotsib = [send(there, there, sibling)]
+
+    pg_c, pu_c, pd_c = summed(s1, r1, rs1)
+    ag1 = gather_z(a1, (pg_c, pu_c, pd_c))
+    gc, uc, wc = gs[y, z], us[y, z], wts[y, z]
+    ys1 = plane_start(
+        st1, sty1,
+        [fold(col_sum(pg_c * pg_c)), fold(col_sum(pu_c * pu_c))]
+        + cut(col_sum(pd_c * pd_c)) + cut(col_sum(wc * pd_c)) + cut(col_sum(wc * wc)),
+    )
 
     zs1 = plane_finish(ys1, sty1, sts1, stz1)
-
+    ky = to_y(kc)
+    ty = to_y(tc)
+
+    qsib += open_blocks(q2, qc, qy)
+    arrived(otsends)
+    for d in y_order:
+        coty[d].wait_recv()
+        first_block = 2 * lax.rem(y + NY - d, NY)
+        for j in (0, 1):
+            block = first_block + j
+            scale = as_columns(otops[c, block][0:1], 2)
+            for i, part in enumerate(halves(decode(oc[block, :, half(c)]) * scale)):
+                o2[block, i, :, half(c)] = part
+        there = o2.at[pl.ds(first_block, 2), :, :, half(c)]
+        cotsib.append(send(there, there, sibling))
+    arrived(tsends)
+    k_scale, t_scale, q_scale = (scale_row(i) for i in range(3))
     arrived(qsib)
-    open_blocks(q2, qc, 1 - c)
-    q_scale = scale_row(2)
-    for d, copy in zip(y_order, coty):
-        copy.wait_recv()
-        there = oc.at[pl.ds(2 * lax.rem(y + NY - d, NY), 2), :, half(c)]
-        cotsib.append(send(there, there, sibling))
-
-    def open_cot(core):
-        for d in (1, 2, 3, 0) if core is not c else (1, 2, 3):
-            for j in (0, 1):
-                block = 2 * lax.rem(y + d, NY) + j
-                scale = as_columns(otops[core, block][0:1], 2)
-                hi, lo = halves(decode(oc[block, :, half(core)]) * scale)
-                o2[block, 0, :, half(core)] = hi
-                o2[block, 1, :, half(core)] = lo
-
-    arrived(otsends)
-    open_cot(c)
     arrived(cotsib)
-    open_cot(1 - c)
     arrived(zs1)
     arrived(ag1)
 
@@ -466,11 +465,20 @@
         acts_q = jnp.concatenate([hcot * linear * dsilu, hcot * act], axis=0)
         cgu = three(dot_nn, q_scale * acts_q, *whole(q2))
         cd = three(dot_nn, act * linear, *whole(o2))
-        fill(s2, c2, cgu, cd)
+        fill(s2, c2, [v.reshape(NZ, 8, D) for v in (cgu[:FS], cgu[FS:], cd)])
     rs2 = scatter_z(c2, r2)
+    def to_sibling(part, sib):
+        copies = {}
+        for d in (2, 1, 3, 0):
+            to = lax.rem(y + d, NY)
+            copies[d] = send(part.at[to, 1 - c], sib.at[to], sibling)
+        return copies
+
     with jax.named_scope("query_grad"):
         part_q[...] = back(acts_q, ren_gu).reshape(NY, 2, TOK, D)
-    sibq = send(part_q.at[:, 1 - c], sib_q, sibling)
+    sibq = to_sibling(part_q, sib_q)
+    ksib = open_blocks(k2, kc, ky)
+    tsib = open_blocks(t2, tc, ty)
 
     cg_c, cu_c, cd_c = summed(s2, r2, rs2)
     ag2 = gather_z(a2, (cg_c, cu_c, cd_c))
@@ -489,35 +497,42 @@
         + cut(col_sum((wc - pd_c * k_d) * cd_c)) + cut(col_sum(pd_c * cd_c)),
     )
 
-    def to_owner(part, sib, plain, codes, scales, rec, rec_scales, copy):
-        copy.wait_recv()
-        value = part[:, c] + sib[...]
-        plain[...] = value
-        top = row_top(value)
-        codes[...] = encode(value, top)
-        for i in range(NY):
-            scales[i] = jnp.broadcast_to(as_row(top[i] * (1.0 / SPAN)), (8, TOK))
-        sends = []
-        for d in y_order:
+    def to_owner(part, sib, plain, codes, scales, rec, rec_scales, copies):
+        sends = {}
+        for d in (2, 1, 3):
             to = lax.rem(y + d, NY)
-            sends.append(
-                (
-                    send(codes.at[to], rec.at[y], at_y(d)),
-                    send(scales.at[to], rec_scales.at[y], at_y(d)),
-                )
+            copies[d].wait_recv()
+            value = part[to, c] + sib[to]
+            top = row_top(value)
+            codes[to] = encode(value, top)
+            scales[to] = jnp.broadcast_to(as_row(top * STEP), (8, TOK))
+            sends[d] = (
+                send(codes.at[to], rec.at[y], at_y(d)),
+                send(scales.at[to], rec_scales.at[y], at_y(d)),
             )
+        copies[0].wait_recv()
+        plain[...] = part[y, c] + sib[y]
         return sends
 
     def owned(plain, rec, rec_scales, copies):
-        value = plain[y]
-        for d, pair in zip(y_order, copies):
-            arrived(pair)
+        value = plain[...]
+        for d in (1, 3, 2):
+            arrived(copies[d])
             src = lax.rem(y + NY - d, NY)
             value = value + decode(rec[src]) * as_columns(rec_scales[src][0:1], 4)
         return value
 
     yq = to_owner(part_q, sib_q, sum_q, code_q, ctop_q, rec_q, rtop_q, sibq)
     zs2 = plane_finish(ys2, sty2, sts2, stz2)
+    arrived(ksib)
+    arrived(tsib)
+    with jax.named_scope("key_products"):
+        both = k_scale * three(
+            dot_nt, jnp.concatenate([flat(gs), flat(us)], axis=0), *whole(k2)
+        )
+        before_s[...] = both[:FS]
+        linear_s[...] = both[FS:]
+        hgrad_s[...] = t_scale * three(dot_nt, flat(wts), *whole(t2))
 
     arrived(zs2)
     arrived(ag2)
@@ -551,12 +566,12 @@
             jnp.concatenate([act * linear, d_h], axis=0),
             jnp.concatenate([dir_d, w_m], axis=0),
         ).reshape(NY, 2, TOK, D)
-        sibt = send(part_t.at[:, 1 - c], sib_t, sibling)
+        sibt = to_sibling(part_t, sib_t)
         part_k[...] = back(
             jnp.concatenate([hgrad * linear * dsilu, hgrad * act, d_b, d_l], axis=0),
             jnp.concatenate([dir_g, dir_u, g_m, u_m], axis=0),
         ).reshape(NY, 2, TOK, D)
-        sibk = send(part_k.at[:, 1 - c], sib_k, sibling)
+        sibk = to_sibling(part_k, sib_k)
         yt = to_owner(part_t, sib_t, sum_t, code_t, ctop_t, rec_t, rtop_t, sibt)
         th_d = three(dot_nn, t_scale * d_h, *whole(t2))
         th_d = th_d + jnp.where(z == 0, direct_d, jnp.zeros_like(direct_d))
@@ -600,7 +615,7 @@
         copy.wait_recv()
         codes = r3[lax.rem(z + NZ - d, NZ)]
         gate_up = gate_up + decode(codes[:, 0:512]) * (
-            codes[:, 512:640].astype(F32)[:, 0:1] * (1.0 / SPAN)
+            codes[:, 512:640].astype(F32)[:, 0:1] * STEP
         )
     gg_ref[...] = gate_up[0:8] + direct_g
     ug_ref[...] = gate_up[8:16] + direct_u
@@ -613,12 +628,8 @@
 
 
 def hand_over(*refs):
-    sems = refs[-1]
-    copies = [pltpu.make_async_copy(refs[i], refs[6 + i], sems.at[i]) for i in range(6)]
-    for copy in copies:
-        copy.start()
-    for copy in copies:
-        copy.wait()
+    for i in range(6):
+        refs[6 + i][...] = refs[i][...]
 
 
 def body(queries, keys, values, rates, gate_fast, up_fast, down_fast, out_proj, out_grad):
@@ -633,7 +644,7 @@
         buf(16, 128), buf(8, 16, 128), buf(16, 128), buf(NZ, 16, 128),
     ]
     grads = [
-        buf(NY, 2, TOK, D), buf(NY, TOK, D), buf(NY, TOK, D),
+        buf(NY, 2, TOK, D), buf(NY, TOK, D), buf(TOK, D),
         buf(NY, TOK, D, dtype=BF16), buf(NY, 8, TOK),
         buf(NY, TOK, D, dtype=BF16), buf(NY, 8, TOK),
     ]
@@ -643,16 +654,18 @@
         + [jax.ShapeDtypeStruct((8, D), F32)] * 3,
         in_specs=[vmem] * 4 + [hbm] * 3 + [vmem] * 2,
         out_specs=[vmem] * 6,
-        scratch_shapes=[buf(8, 2, TOK, D, dtype=BF16)] * 4
+        scratch_shapes=[buf(2, 2, TOK, D, dtype=BF16)] * 2
+        + [buf(8, 2, TOK, D, dtype=BF16)] * 4
         + [buf(8, TOK, D, dtype=BF16)] * 4
         + [
             buf(8, TOK), buf(8, 8, TOK), buf(2, 8, 8, TOK),
             buf(64, 256, dtype=BF16),
             buf(NZ, 512, 256, dtype=BF16),
             buf(NX, 256, 1024, dtype=BF16),
-            buf(NZ, 8, D), buf(NZ, 8, D), buf(D, 128), buf(NZ, 8, D),
+            buf(NY, NZ, 8, D), buf(NY, NZ, 8, D), buf(D, D), buf(NY, NZ, 8, D),
         ]
         + [buf(FS, 8 * TOK)] * 3
+        + [buf(3, NY, NZ, 8, D), *[buf(NY, NZ, 16, 896, dtype=BF16)] * 2]
         + exchange
         + exchange
         + [
@@ -672,9 +685,8 @@
     outs = pl.pallas_call(
         hand_over,
         out_shape=[jax.ShapeDtypeStruct(o.shape, F32) for o in outs],
-        in_specs=[hbm] * 6,
-        out_specs=[hbm] * 6,
-        scratch_shapes=[pltpu.SemaphoreType.DMA((6,))],
+        in_specs=[vmem] * 6,
+        out_specs=[vmem] * 6,
     )(*outs)
     return (*outs[:3], *(o.reshape(1, 8, D) for o in outs[3:]))
 

time: 128 us -> 103 us (0.80)
  Pallas kernels: 127 us -> 102 us
    pallas_call x1, Pallas kernels: 26.5 us -> 2.04 us  [body(): pl.pallas_call(hand_over, out_shape=[jax.ShapeDtypeStruct(o.shape, F32) f...]
where the time goes in v2:
time: 103 us
  Pallas kernels  102 us (99%)
    pallas_call x1, Pallas kernels, body(): pl.pallas_call(kernel, out_shape=[jax.ShapeDtypeStruct((TOK, D), F32)] *...  100 us

profile of v2, /device:TPU:1, one launch (start us, length us, event | category | flops | bytes accessed | tf_op | source)
XLA Modules:
  0.0 102.8 jit_solution(3690150152371892850)
XLA Ops:
  0.6 100.2 %shard_map.136 = (f32[128,512]{1,0:T(8,128)}, f32[128,512]{1,0:T(8,128)}, f32[128,512]{1,0:T(8,128)}, f32[8,512]{1,0:T(8,128)}, f32[8,512]{1,0:T(8,128)}, /*index=5*/f32[8,512]{1,0:T(8,128)}) custom-call(f32[128,512]{1,0:T(8,128)} %q_ref.1, f32[128,512]{1,0:T(8,128)} %k_ref.1, f32[128,512]{1,0:T(8,128)} %v_ref.1, f32[1,128]{1,0:T(1,128)} %rate_ref.1, ...), custom_call_target="tpu_custom_call" | custom-call | tf_op jit(solution)/shard_map/pallas_call | solution.py:651
  100.8 2.0 %shard_map.137 = (f32[128,512]{1,0:T(8,128)}, f32[128,512]{1,0:T(8,128)}, f32[128,512]{1,0:T(8,128)}, f32[8,512]{1,0:T(8,128)}, f32[8,512]{1,0:T(8,128)}, /*index=5*/f32[8,512]{1,0:T(8,128)}) custom-call(f32[128,512]{1,0:T(8,128)} %get-tuple-element.18.refs_0_, f32[128,512]{1,0:T(8,128)} %get-tuple-element.19.refs_1_, f32[128,512]{1,0:T(8,128)} %get-tuple-element.20.refs_2_, ...), custom_call_target="tpu_custom_call" | custom-call | tf_op jit(solution)/shard_map/pallas_call | solution.py:685

commit v3 on v2

--- a/solution.py
+++ b/solution.py
@@ -355,13 +355,13 @@
         return [send(sts, stz.at[z], at_z(d)) for d in z_order]
 
     r3rd = ring(3, r2nd)
-    r4th = ring(4, r3rd)
     mine = [p1[i, y] for i in range(3)]
     for d in (1, 3, 2):
         py[d].wait_recv()
         more = unpack(pr1[lax.rem(y + NY - d, NY)])
         mine = [a + b for a, b in zip(mine, more)]
     fill(s1, c1, mine)
+    r4th = ring(4, r3rd)
     rs1 = scatter_z(c1, r1)
     qy = to_y(qc)
 
@@ -533,6 +533,10 @@
         before_s[...] = both[:FS]
         linear_s[...] = both[FS:]
         hgrad_s[...] = t_scale * three(dot_nt, flat(wts), *whole(t2))
+        before, linear, hgrad = before_s[...], linear_s[...], hgrad_s[...]
+        sigma, act, dsilu = silu_parts(before)
+        curve = sigma * (1.0 - sigma) * (2.0 + before * (1.0 - 2.0 * sigma))
+        hidden, before_grad, linear_grad = act * linear, hgrad * linear * dsilu, hgrad * act
 
     arrived(zs2)
     arrived(ag2)
@@ -556,19 +560,16 @@
         both = k_scale * three(dot_nt, jnp.concatenate([dir_g, dir_u], axis=0), *whole(k2))
         d_bg, d_lg = both[:FS], both[FS:]
         d_hid = t_scale * three(dot_nt, dir_d, *whole(t2))
-        before, linear, hgrad = before_s[...], linear_s[...], hgrad_s[...]
-        sigma, act, dsilu = silu_parts(before)
-        curve = sigma * (1.0 - sigma) * (2.0 + before * (1.0 - 2.0 * sigma))
         d_h = d_bg * linear * dsilu + d_lg * act
         d_l = d_bg * hgrad * dsilu + d_hid * act
         d_b = d_bg * hgrad * linear * curve + (d_lg * hgrad + d_hid * linear) * dsilu
         part_t[...] = back(
-            jnp.concatenate([act * linear, d_h], axis=0),
+            jnp.concatenate([hidden, d_h], axis=0),
             jnp.concatenate([dir_d, w_m], axis=0),
         ).reshape(NY, 2, TOK, D)
         sibt = to_sibling(part_t, sib_t)
         part_k[...] = back(
-            jnp.concatenate([hgrad * linear * dsilu, hgrad * act, d_b, d_l], axis=0),
+            jnp.concatenate([before_grad, linear_grad, d_b, d_l], axis=0),
             jnp.concatenate([dir_g, dir_u, g_m, u_m], axis=0),
         ).reshape(NY, 2, TOK, D)
         sibk = to_sibling(part_k, sib_k)

time: 103 us -> 103 us (level)
  no operation moved by 1% of the time
where the time goes in v3:
time: 103 us
  Pallas kernels  102 us (99%)
    pallas_call x1, Pallas kernels, body(): pl.pallas_call(kernel, out_shape=[jax.ShapeDtypeStruct((TOK, D), F32)] *...  99.8 us

profile of v3, /device:TPU:1, one launch (start us, length us, event | category | flops | bytes accessed | tf_op | source)
XLA Modules:
  0.0 102.5 jit_solution(5700117494771694408)
XLA Ops:
  0.6 99.8 %shard_map.136 = (f32[128,512]{1,0:T(8,128)}, f32[128,512]{1,0:T(8,128)}, f32[128,512]{1,0:T(8,128)}, f32[8,512]{1,0:T(8,128)}, f32[8,512]{1,0:T(8,128)}, /*index=5*/f32[8,512]{1,0:T(8,128)}) custom-call(f32[128,512]{1,0:T(8,128)} %q_ref.1, f32[128,512]{1,0:T(8,128)} %k_ref.1, f32[128,512]{1,0:T(8,128)} %v_ref.1, f32[1,128]{1,0:T(1,128)} %rate_ref.1, ...), custom_call_target="tpu_custom_call" | custom-call | tf_op jit(solution)/shard_map/pallas_call | solution.py:652
  100.5 2.0 %shard_map.137 = (f32[128,512]{1,0:T(8,128)}, f32[128,512]{1,0:T(8,128)}, f32[128,512]{1,0:T(8,128)}, f32[8,512]{1,0:T(8,128)}, f32[8,512]{1,0:T(8,128)}, /*index=5*/f32[8,512]{1,0:T(8,128)}) custom-call(f32[128,512]{1,0:T(8,128)} %get-tuple-element.18.refs_0_, f32[128,512]{1,0:T(8,128)} %get-tuple-element.19.refs_1_, f32[128,512]{1,0:T(8,128)} %get-tuple-element.20.refs_2_, ...), custom_call_target="tpu_custom_call" | custom-call | tf_op jit(solution)/shard_map/pallas_call | solution.py:686
